TPU v7x, 32 devices: a whole 2x2x4 slice. The times are simulated.
32 devices in a mesh: groups: 2 (over y), row: 4 (over z), col: 4 (over x, core).
Axes of the slice: x: 2, y: 2, z: 4, core: 2. Of those that a mesh axis runs over, the one named last changes fastest.
Arguments:
- features: bfloat16 [8, 2048, 256], P(('groups', 'row'), 'col'), parts along dimension 0, may hold values from -6 to 6
- tile_values: bfloat16 [8, 4, 1024, 4096], P(('groups', 'row'), 'col'), parts along dimension 0, may hold values from -0.125 to 0.125
- tile_rows: int32 [8, 4, 1024], P(('groups', 'row'), 'col'), parts along dimension 0, may hold values from 0 to 31
- tile_cols: int32 [8, 4, 1024], P(('groups', 'row'), 'col'), parts along dimension 0, may hold values from 0 to 31
- counts: int32 [8, 4], P(('groups', 'row'), 'col'), parts along dimension 0, may hold values from 128 to 1024, as said below
- weight: bfloat16 [256, 256], replicated, may hold values from -0.375 to 0.375
- bias: float32 [256], replicated, may hold values from -3 to 3
Outputs:
- layer_out: bfloat16 [8, 2048, 256], P(('groups', 'col'), 'row'), parts along dimension 0
There are 2 independent parts, one for each index of `groups`. A program takes and returns all parts, laid end to end along the dimension named above; an argument that names none is the same for every part. Nothing has to cross between parts.
Inputs may be any that keep to these rules, and one draw needn't show every extreme that they name: Slots at or past counts[r, c] hold values that are to be ignored; coordinate pairs may repeat within a cell, and repeated tiles add. In every draw one grid cell has exactly 1024 live slots.
All inputs are finite; a program needn't handle non-finite values.
Results may differ from a plain program's by a relative error of at most 0.0046.
Values may be sent and summed in bfloat16 or wider, within the bound.
A program may use at most 128 MiB of HBM per device.

v0:
```python
import functools

import jax
import jax.numpy as jnp
from jax import lax
from jax.experimental import pallas as pl
from jax.experimental.pallas import tpu as pltpu
from jax.sharding import PartitionSpec as P

TILE = 64
LANES = 128
MESH = pl.DeviceIdType.MESH


def layer_kernel(
    n_row, n_col, live_ref, vals_hbm, rows_ref, cols_ref, feat_ref, weight_ref, bias_ref,
    out_ref, vals, pick, dense, src, swapped, acc, sent, up_in, down_in,
    vals_sem, far_send, far_recv, near_send, near_recv, send_sem, up_sem, down_sem,
):
    steps, slots, lanes = vals.shape
    cuts = far_send.shape[1]
    tiles_in = pick.shape[0]
    piece_rows = feat_ref.shape[1]
    col_tiles = src.shape[0] // TILE
    row_tiles = tiles_in // col_tiles
    half = tiles_in // 2
    chunk = min(half, 512)
    pairs = chunk // row_tiles
    own = row_tiles // n_row
    blocks = lanes // LANES
    chips = n_col // 2
    z = lax.axis_index("row")
    me = lax.axis_index("col")
    core = lax.rem(me, 2)
    sibling = me + 1 - 2 * core

    def load(step):
        return pltpu.make_async_copy(
            vals_hbm.at[0, 0, :, pl.ds(pl.multiple_of(step * lanes, lanes), lanes)],
            vals.at[step], vals_sem.at[step],
        )

    for step in range(steps):
        load(step).start()

    cut_rows = piece_rows // cuts

    def rows_of(index, cut):
        first = pl.multiple_of(index * piece_rows + cut * cut_rows, cut_rows)
        return src.at[pl.ds(first, cut_rows)]

    def far(d, cut):
        return pltpu.make_async_remote_copy(
            src_ref=feat_ref.at[0, pl.ds(cut * cut_rows, cut_rows)], dst_ref=rows_of(me, cut),
            send_sem=far_send.at[d, cut], recv_sem=far_recv.at[d, cut],
            device_id={"col": lax.rem(me + 2 * d, n_col)}, device_id_type=MESH,
        )

    def near(d, cut):
        origin = lax.rem(me + n_col - 2 * d, n_col)
        mine = feat_ref.at[0, pl.ds(cut * cut_rows, cut_rows)]
        return pltpu.make_async_remote_copy(
            src_ref=mine if d == 0 else rows_of(origin, cut), dst_ref=rows_of(origin, cut),
            send_sem=near_send.at[d, cut], recv_sem=near_recv.at[d, cut],
            device_id={"col": sibling}, device_id_type=MESH,
        )

    def passed(p, o, to, sem):
        landing = up_in if sem is up_sem else down_in
        return pltpu.make_async_remote_copy(
            src_ref=sent.at[p, o], dst_ref=landing.at[p, o],
            send_sem=send_sem.at[p, o], recv_sem=sem.at[p, o],
            device_id={"row": to}, device_id_type=MESH,
        )

    barrier = pltpu.get_barrier_semaphore()
    for d in range(1, chips):
        pl.semaphore_signal(
            barrier, inc=1, device_id={"col": lax.rem(me + 2 * d, n_col)}, device_id_type=MESH
        )
    pl.semaphore_signal(barrier, inc=1, device_id={"col": sibling}, device_id_type=MESH)

    @pl.when(z > 0)
    def _():
        pl.semaphore_signal(barrier, inc=1, device_id={"row": z - 1}, device_id_type=MESH)

    @pl.when(z < n_row - 1)
    def _():
        pl.semaphore_signal(barrier, inc=1, device_id={"row": z + 1}, device_id_type=MESH)

    beside = lax.div(z + n_row - 1, n_row) + lax.div(2 * n_row - 2 - z, n_row)
    pl.semaphore_wait(barrier, chips + beside)

    for d in range(1, chips):
        for cut in range(cuts):
            far(d, cut).start()
    for cut in range(cuts):
        near(0, cut).start()
    src[pl.ds(pl.multiple_of(me * piece_rows, piece_rows), piece_rows), :] = feat_ref[0]

    slot = lax.broadcasted_iota(jnp.int32, (1, slots), 1)
    place = (cols_ref[0] & 1) * half + (cols_ref[0] >> 1) * row_tiles + rows_ref[0]
    place = jnp.where(slot < live_ref[0, 0], place, -1)

    @pl.loop(0, tiles_in // 128)
    def _(at):
        first = pl.multiple_of(at * 128, 128)
        index = first + lax.broadcasted_iota(jnp.int32, (128, slots), 0)
        pick[pl.ds(first, 128), :] = jnp.where(index == place, 1.0, 0.0).astype(jnp.bfloat16)

    is_low = lax.broadcasted_iota(jnp.int32, (row_tiles, LANES), 1) < TILE

    def densify(step):
        def one_chunk(at, carry):
            first = pl.multiple_of(at * chunk, chunk)
            for sub in range(lanes // 256):
                block_vals = vals[step, :, sub * 256 : (sub + 1) * 256]
                even = jnp.dot(
                    pick[pl.ds(first, chunk), :], block_vals,
                    preferred_element_type=jnp.float32,
                )
                odd = jnp.dot(
                    pick[pl.ds(half + first, chunk), :], block_vals,
                    preferred_element_type=jnp.float32,
                )
                for part in range(2):
                    block = 2 * sub + part
                    cut = slice(part * LANES, (part + 1) * LANES)
                    for pair in range(pairs):
                        down = slice(pair * row_tiles, (pair + 1) * row_tiles)
                        held = even[down, cut]
                        turned = pltpu.roll(odd[down, cut], TILE, 1)
                        lane = pl.multiple_of((at * pairs + pair) * LANES, LANES)
                        where = pl.ds(block * row_tiles, row_tiles), pl.ds(lane, LANES)
                        dense[(0,) + where] = jnp.where(is_low, held, turned).astype(jnp.bfloat16)
                        dense[(1,) + where] = jnp.where(is_low, turned, held).astype(jnp.bfloat16)
            return carry

        if half == chunk:
            one_chunk(0, 0)
        else:
            lax.fori_loop(0, half // chunk, one_chunk, 0)

    def finish_gather():
        for d in range(1, chips):
            for cut in range(cuts):
                far(d, cut).wait_recv()
                near(d, cut).start()
        for d in range(chips):
            for cut in range(cuts):
                near(d, cut).wait_recv()
        for pair in range(col_tiles // 2):
            low = 2 * pair * TILE
            swapped[low : low + TILE, :] = src[low + TILE : low + 2 * TILE, :]
            swapped[low + TILE : low + 2 * TILE, :] = src[low : low + TILE, :]

    def multiply(step):
        for parity, source in ((0, src), (1, swapped)):
            sums = jnp.dot(dense[parity], source[...], preferred_element_type=jnp.float32)
            for block in range(blocks):
                for owner in range(n_row):
                    low = block * row_tiles + owner * own
                    to = (2 * block + parity) * own
                    acc[step, owner, to : to + own, :] = sums[low : low + own, :]

    def pass_on(p, is_first, sem, landing, to, owner_of, begin, end):
        def one(j, carry):
            o = owner_of(j)

            @pl.when(is_first)
            def _():
                sent[p, o] = acc[p, o].astype(jnp.bfloat16)

            @pl.when(jnp.logical_not(is_first))
            def _():
                passed(p, o, to, sem).wait_recv()
                sent[p, o] = (acc[p, o] + landing[p, o].astype(jnp.float32)).astype(jnp.bfloat16)

            passed(p, o, to, sem).start()
            return carry

        lax.fori_loop(begin, end, one, 0)

    above_count = n_row - 1 - z
    below_count = z
    above_early = jnp.minimum(above_count, jnp.maximum(above_count - 1, 1))
    below_early = jnp.minimum(below_count, jnp.maximum(below_count - 1, 1))

    def pass_up(p, begin, end):
        pass_on(p, z == 0, up_sem, up_in, z + 1, lambda j: n_row - 1 - j, begin, end)

    def pass_down(p, begin, end):
        pass_on(p, z == n_row - 1, down_sem, down_in, z - 1, lambda j: j, begin, end)

    def one_step(t, carry):
        @pl.when(t < steps)
        def _():
            load(t).wait()
            densify(t)

            @pl.when(t == 0)
            def _():
                finish_gather()

            multiply(t)

        up = t - z

        @pl.when(jnp.logical_and(up >= 0, up < steps))
        def _():
            pass_up(up, 0, above_early)

        below = t - (n_row - 1 - z)

        @pl.when(jnp.logical_and(below >= 0, below < steps))
        def _():
            pass_down(below, 0, below_early)

        return carry

    lax.fori_loop(0, steps + n_row - 1, one_step, 0)

    def late(p, carry):
        pass_up(p, above_early, above_count)
        pass_down(p, below_early, below_count)
        return carry

    lax.fori_loop(0, steps, late, 0)

    def collect(p, carry):
        @pl.when(z > 0)
        def _():
            passed(p, z, z + 1, up_sem).wait_recv()
            acc[p, z] = acc[p, z] + up_in[p, z].astype(jnp.float32)

        @pl.when(z < n_row - 1)
        def _():
            passed(p, z, z - 1, down_sem).wait_recv()
            acc[p, z] = acc[p, z] + down_in[p, z].astype(jnp.float32)

        return carry

    lax.fori_loop(0, steps, collect, 0)

    hidden = jnp.concatenate([acc[p, z].astype(jnp.bfloat16) for p in range(steps)], axis=0)
    target = lax.broadcasted_iota(jnp.int32, (piece_rows, piece_rows), 0)
    origin = lax.broadcasted_iota(jnp.int32, (piece_rows, piece_rows), 1)
    wanted = (target & (TILE - 1)) * own + (target >> 6)
    order = jnp.where(origin == wanted, 1.0, 0.0).astype(jnp.bfloat16)
    hidden = jnp.dot(order, hidden, preferred_element_type=jnp.float32).astype(jnp.bfloat16)
    mixed = jnp.dot(hidden, weight_ref[...], preferred_element_type=jnp.float32) + bias_ref[...]
    out_ref[0] = jnp.maximum(mixed, 0.0).astype(jnp.bfloat16)

    for d in range(1, chips):
        for cut in range(cuts):
            far(d, cut).wait_send()
    for d in range(chips):
        for cut in range(cuts):
            near(d, cut).wait_send()

    def drain(p, carry):
        def up_one(o, inner):
            passed(p, o, z + 1, up_sem).wait_send()
            return inner

        def down_one(o, inner):
            passed(p, o, z - 1, down_sem).wait_send()
            return inner

        lax.fori_loop(z + 1, n_row, up_one, 0)
        lax.fori_loop(0, z, down_one, 0)
        return carry

    lax.fori_loop(0, steps, drain, 0)


def on_device(features, tile_values, tile_rows, tile_cols, counts, weight, bias):
    n_row, n_col = lax.axis_size("row"), lax.axis_size("col")
    piece_rows, width = features.shape[1:]
    slots, entries = tile_values.shape[2:]
    own = piece_rows // TILE
    row_tiles = n_row * own
    source_rows = n_col * piece_rows
    tiles_in = row_tiles * source_rows // TILE
    steps = 2 if tiles_in <= 2048 else 8
    lanes = entries // steps
    blocks = lanes // LANES
    part_rows = 2 * blocks * own
    vmem = pl.BlockSpec(memory_space=pltpu.VMEM)
    slabs = (steps, n_row, part_rows, width)
    dma = pltpu.SemaphoreType.DMA
    return pl.pallas_call(
        functools.partial(layer_kernel, n_row, n_col),
        in_specs=[
            pl.BlockSpec(memory_space=pltpu.SMEM), pl.BlockSpec(memory_space=pl.ANY),
            vmem, vmem, vmem, vmem, vmem,
        ],
        out_specs=vmem,
        out_shape=jax.ShapeDtypeStruct((1, piece_rows, width), jnp.bfloat16),
        scratch_shapes=[
            pltpu.VMEM((steps, slots, lanes), jnp.bfloat16),
            pltpu.VMEM((tiles_in, slots), jnp.bfloat16),
            pltpu.VMEM((2, blocks * row_tiles, source_rows), jnp.bfloat16),
            pltpu.VMEM((source_rows, width), jnp.bfloat16),
            pltpu.VMEM((source_rows, width), jnp.bfloat16),
            pltpu.VMEM(slabs, jnp.float32),
            pltpu.VMEM(slabs, jnp.bfloat16),
            pltpu.VMEM(slabs, jnp.bfloat16),
            pltpu.VMEM(slabs, jnp.bfloat16),
            dma((steps,)), dma((n_col // 2, 4)), dma((n_col // 2, 4)),
            dma((n_col // 2, 4)), dma((n_col // 2, 4)),
            dma((steps, n_row)), dma((steps, n_row)), dma((steps, n_row)),
        ],
        compiler_params=pltpu.CompilerParams(
            collective_id=0, has_side_effects=True, vmem_limit_bytes=62 * 1024 * 1024
        ),
    )(counts, tile_values, tile_rows, tile_cols, features, weight, bias.reshape(1, width))


def solution(mesh):
    in_specs = (
        P(("groups", "row"), "col", None),
        P(("groups", "row"), "col", None, None),
        P(("groups", "row"), "col", None),
        P(("groups", "row"), "col", None),
        P(("groups", "row"), "col"),
        P(),
        P(),
    )
    out_specs = P(("groups", "col"), "row", None)
    return jax.shard_map(
        on_device, mesh=mesh, in_specs=in_specs, out_specs=out_specs, check_vma=False
    )
```

profile of v0, /device:TPU:0, one launch (start us, length us, event | category | flops | bytes accessed | tf_op | source)
XLA Modules:
  0.0 39.7 jit_solution(15061713892548867755)
XLA Ops:
  0.7 37.4 %shard_map.73 = bf16[1,512,256]{2,1,0:T(8,128)(2,1)} custom-call(s32[1,1]{1,0:T(1,128)S(6)} %copy.9.live_ref, bf16[1,1,1024,4096]{3,2,1,0:T(8,128)(2,1)} %vals_hbm.1, s32[1,1,1024]{2,1,0:T(1,128)} %rows_ref.1, s32[1,1,1024]{2,1,0:T(1,128)} %cols_ref.1, bf16[1,512,256]{2,1,0:T(8,128)(2,1)} %feat_ref.1, bf16[256,256]{1,0:T(8,128)(2,1)} %weight_ref.1, ...), custom_call_target="tpu_custom_call" | custom-call | tf_op jit(solution)/shard_map/pallas_call | solution.py:292
  38.0 1.7 %copy.10 = bf16[1,512,256]{2,1,0:T(8,128)(2,1)} copy(bf16[1,512,256]{2,1,0:T(8,128)(2,1)} %shard_map.73) | data formatting | bytes 524288
where the time goes:
time: 40.2 us; the launch traced here: 39.7 us
  Pallas kernels  37.4 us (93%)
  local copies, waits for them, and re-layouts  1.67 us (4%)
  between operations  0.66 us (2%)
    pallas_call x1, Pallas kernels, on_device(): pl.pallas_call(functools.partial(layer_kernel, n_row, n_col), in_specs=[p...  37.4 us
    unnamed x1, local copies, waits for them, and re-layouts  1.67 us

commit v1 on v0

v1 whole, which is shorter than its diff:
```python
import functools

import jax
import jax.numpy as jnp
from jax import lax
from jax.experimental import pallas as pl
from jax.experimental.pallas import tpu as pltpu
from jax.sharding import PartitionSpec as P

TILE = 64
LANES = 128
FINAL = 16
LAG = 2
PLAN = (
    "d00", "d01", "d10", "r00", "d11", "s00", "m00", "x00", "m10", "r10", "x10", "l00",
    "l10", "d20", "d21", "m20", "x20", "f00", "s10", "m01", "x01", "f10", "m11", "x11",
    "m21", "x21", "d30", "f20", "d31", "f01", "m30", "x30", "m31", "x31", "f11", "f21",
    "f30", "f31", "l20", "l01", "l11", "l21", "l30", "l31",
)
MESH = pl.DeviceIdType.MESH


def layer_kernel(
    n_row, n_col, piece, counts_hbm, vals_hbm, rows_hbm, cols_hbm, feat_hbm, weight_hbm, bias_hbm,
    out_ref, vals, live, rows_in, cols_in, weight, bias, pick, dense, src, wide, acc, up_in, down_in,
    final, vals_sem, small_sem, own_sem, far_send, far_recv, near_send, near_recv, send_sem, up_sem,
    down_sem,
):
    steps, slots, lanes = vals.shape
    halves, source_rows, part = src.shape
    cuts = far_send.shape[2]
    tiles_in = pick.shape[0]
    piece_rows = feat_hbm.shape[1]
    col_tiles = source_rows // TILE
    row_tiles = tiles_in // col_tiles
    chunk = min(tiles_in, 1024)
    chunk_cols = chunk // row_tiles
    own = row_tiles // n_row
    blocks = lanes // LANES
    units = steps * halves
    chips = n_col // 2
    z = lax.axis_index("row")
    me = lax.axis_index("col")
    core = lax.rem(me, 2)
    sibling = me + 1 - 2 * core

    barrier = pltpu.get_barrier_semaphore()
    for d in range(1, chips):
        pl.semaphore_signal(
            barrier, inc=1, device_id={"col": lax.rem(me + 2 * d, n_col)}, device_id_type=MESH
        )
    pl.semaphore_signal(barrier, inc=1, device_id={"col": sibling}, device_id_type=MESH)

    direct = n_row == 4
    reach = 2 if direct else 1
    for d in range(1, reach + 1):

        @pl.when(z >= d)
        def _():
            pl.semaphore_signal(barrier, inc=1, device_id={"row": z - d}, device_id_type=MESH)

        @pl.when(z < n_row - d)
        def _():
            pl.semaphore_signal(barrier, inc=1, device_id={"row": z + d}, device_id_type=MESH)

    smalls = [
        pltpu.make_async_copy(rows_hbm.at[0], rows_in, small_sem.at[0]),
        pltpu.make_async_copy(cols_hbm.at[0], cols_in, small_sem.at[1]),
        pltpu.make_async_copy(counts_hbm, live, small_sem.at[2]),
        pltpu.make_async_copy(weight_hbm, weight, small_sem.at[3]),
        pltpu.make_async_copy(bias_hbm, bias, small_sem.at[4]),
    ]
    cut_rows = piece_rows // cuts

    def rows_of(index, q, cut):
        first = pl.multiple_of(index * piece_rows + cut * cut_rows, cut_rows)
        return src.at[q, pl.ds(first, cut_rows)]

    def far(d, q, cut):
        return pltpu.make_async_remote_copy(
            src_ref=rows_of(me, q, cut), dst_ref=rows_of(me, q, cut),
            send_sem=far_send.at[d, q, cut], recv_sem=far_recv.at[d, q, cut],
            device_id={"col": lax.rem(me + 2 * d, n_col)}, device_id_type=MESH,
        )

    def near(d, q, cut):
        origin = lax.rem(me + n_col - 2 * d, n_col)
        return pltpu.make_async_remote_copy(
            src_ref=rows_of(origin, q, cut), dst_ref=rows_of(origin, q, cut),
            send_sem=near_send.at[d, q, cut], recv_sem=near_recv.at[d, q, cut],
            device_id={"col": sibling}, device_id_type=MESH,
        )

    def keep(q):
        return pltpu.make_async_copy(
            feat_hbm.at[0, :, pl.ds(q * part, part)],
            src.at[q, pl.ds(pl.multiple_of(me * piece_rows, piece_rows), piece_rows)],
            own_sem.at[q],
        )

    for q in range(halves):
        keep(q).start()
    for copy in smalls[:3]:
        copy.start()

    def load(step):
        return pltpu.make_async_copy(
            vals_hbm.at[0, 0, :, pl.ds(pl.multiple_of(step * lanes, lanes), lanes)],
            vals.at[step], vals_sem.at[step],
        )

    for step in range(steps):
        load(step).start()
    beside = jnp.minimum(z, reach) + jnp.minimum(n_row - 1 - z, reach)
    pl.semaphore_wait(barrier, chips + beside)

    for q in range(halves):
        keep(q).wait()
        for cut in range(cuts):
            for d in range(1, chips):
                far(d, q, cut).start()
            near(0, q, cut).start()
    for copy in smalls[3:]:
        copy.start()
    for copy in smalls[:3]:
        copy.wait()

    slot = lax.broadcasted_iota(jnp.int32, (1, slots), 1)
    place = cols_in[...] * row_tiles + rows_in[...]
    place = jnp.where(slot < live[...], place, -1)

    @pl.loop(0, tiles_in // 128)
    def _(at):
        first = pl.multiple_of(at * 128, 128)
        index = first + lax.broadcasted_iota(jnp.int32, (128, slots), 0)
        pick[pl.ds(first, 128), :] = jnp.where(index == place, 1.0, 0.0).astype(jnp.bfloat16)

    @pl.loop(0, col_tiles)
    def _(c):
        low = pl.multiple_of(c * 2 * TILE, 2 * TILE)
        for q in range(halves):
            wide[q, pl.ds(low, TILE), part:] = jnp.zeros((TILE, part), jnp.bfloat16)
            wide[q, pl.ds(low + TILE, TILE), :part] = jnp.zeros((TILE, part), jnp.bfloat16)

    def densify(step, held, at_piece):
        def one_chunk(at, carry):
            first = pl.multiple_of(at * chunk, chunk)
            for low in range(at_piece * piece, (at_piece + 1) * piece, 256):
                sums = jnp.dot(
                    pick[pl.ds(first, chunk), :], vals[step, :, low : low + 256],
                    preferred_element_type=jnp.float32,
                ).astype(jnp.bfloat16)
                for block in range(2):
                    down = pl.ds((low // LANES + block) * row_tiles, row_tiles)
                    for c in range(chunk_cols):
                        lane = pl.multiple_of((at * chunk_cols + c) * LANES, LANES)
                        dense[held, down, pl.ds(lane, LANES)] = sums[
                            c * row_tiles : (c + 1) * row_tiles,
                            block * LANES : (block + 1) * LANES,
                        ]
            return carry

        if chunk == tiles_in:
            one_chunk(0, 0)
        else:
            lax.fori_loop(0, tiles_in // chunk, one_chunk, 0)

    def relay(q):
        for d in range(1, chips):
            for cut in range(cuts):
                far(d, q, cut).wait_recv()
                near(d, q, cut).start()

    def spread(q):
        for d in range(chips):
            for cut in range(cuts):
                near(d, q, cut).wait_recv()

        @pl.loop(0, col_tiles, unroll=4)
        def _(c):
            rows = src[q, pl.ds(pl.multiple_of(c * TILE, TILE), TILE), :]
            low = pl.multiple_of(c * 2 * TILE, 2 * TILE)
            wide[q, pl.ds(low, TILE), :part] = rows
            wide[q, pl.ds(low + TILE, TILE), part:] = rows

    def multiply(unit, held, q):
        sums = jnp.dot(dense[held], wide[q], preferred_element_type=jnp.float32)
        for block in range(blocks):
            for owner in range(n_row):
                low = block * row_tiles + owner * own
                for side in range(2):
                    to = (2 * block + side) * own
                    acc[unit, owner, to : to + own, :] = sums[
                        low : low + own, side * part : (side + 1) * part
                    ]

    def passed(u, o, to, is_up):
        land, sem = (up_in, up_sem) if is_up else (down_in, down_sem)
        return pltpu.make_async_remote_copy(
            src_ref=land.at[u, o], dst_ref=land.at[u, o],
            send_sem=send_sem.at[u, o], recv_sem=sem.at[u, o],
            device_id={"row": to}, device_id_type=MESH,
        )

    def pass_on(u, is_first, is_up, to, owner_of, begin, end):
        land = up_in if is_up else down_in

        def one(j, carry):
            o = owner_of(j)

            @pl.when(is_first)
            def _():
                land[u, o] = acc[u, o].astype(jnp.bfloat16)

            @pl.when(jnp.logical_not(is_first))
            def _():
                passed(u, o, to, is_up).wait_recv()
                land[u, o] = (acc[u, o] + land[u, o].astype(jnp.float32)).astype(jnp.bfloat16)

            passed(u, o, to, is_up).start()
            return carry

        lax.fori_loop(begin, end, one, 0)

    late_from = units // 2
    above_count = n_row - 1 - z
    below_count = z
    above_early = jnp.minimum(above_count, jnp.maximum(above_count - 1, 1))
    below_early = jnp.minimum(below_count, jnp.maximum(below_count - 1, 1))

    def pass_up(u, begin, end):
        pass_on(u, z == 0, True, z + 1, lambda j: n_row - 1 - j, begin, end)

    def pass_down(u, begin, end):
        pass_on(u, z == n_row - 1, False, z - 1, lambda j: j, begin, end)

    def chain_exchange(t):
        up = t - LAG * z

        @pl.when(jnp.logical_and(up >= 0, up < units))
        def _():
            pass_up(up, 0, jnp.where(up < late_from, above_count, above_early))

        below = t - LAG * (n_row - 1 - z)

        @pl.when(jnp.logical_and(below >= 0, below < units))
        def _():
            pass_down(below, 0, jnp.where(below < late_from, below_count, below_early))

    is_end = jnp.logical_or(z == 0, z == n_row - 1)
    is_low = z < 2
    end_of = jnp.where(is_low, 0, n_row - 1)
    middle_of = jnp.where(is_low, 1, n_row - 2)
    far_middle = n_row - 1 - middle_of
    far_end = n_row - 1 - end_of

    def sent(u, o, to, at):
        return pltpu.make_async_remote_copy(
            src_ref=down_in.at[u, o], dst_ref=up_in.at[u, at],
            send_sem=send_sem.at[u, o], recv_sem=up_sem.at[u, at],
            device_id={"row": to}, device_id_type=MESH,
        )

    def send(u, o, to, at):
        down_in[u, o] = acc[u, o].astype(jnp.bfloat16)
        sent(u, o, to, at).start()

    def first_sends(u):
        @pl.when(is_end)
        def _():
            send(u, far_end, middle_of, middle_of)
            send(u, far_middle, middle_of, far_end)

        @pl.when(jnp.logical_not(is_end))
        def _():
            send(u, end_of, end_of, z)

    def forward(u):
        @pl.when(jnp.logical_not(is_end))
        def _():
            for o, at in ((far_end, z), (far_middle, far_end)):
                sent(u, far_end, far_end, at).wait_recv()
                down_in[u, o] = (
                    acc[u, o] + up_in[u, at].astype(jnp.float32)
                ).astype(jnp.bfloat16)
                sent(u, o, o, z).start()

    def last_sends(u):
        @pl.when(is_end)
        def _():
            send(u, middle_of, middle_of, z)

    pieces = lanes // piece

    def one_step(step, carry):
        load(step).wait()
        for k in range(pieces):
            densify(step, 0, k)

        @pl.when(step == 0)
        def _():
            for q in range(halves):
                relay(q)
                spread(q)

        for q in range(halves):
            multiply(step * halves + q, 0, q)
            chain_exchange(step * halves + q)
        return carry

    def rest(t, carry):
        chain_exchange(t)
        return carry

    def late(u, carry):
        pass_up(u, above_early, above_count)
        pass_down(u, below_early, below_count)
        return carry

    if direct:
        for action in PLAN:
            what, at, k = action[0], int(action[1]), int(action[2])
            unit = at * halves + k
            if what == "d":
                if k == 0:
                    load(at).wait()
                densify(at, at, k)
            elif what == "r":
                relay(at)
            elif what == "s":
                spread(at)
            elif what == "m":
                multiply(unit, at, k)
            elif what == "x":
                first_sends(unit)
            elif what == "f":
                forward(unit)
            elif what == "l":
                last_sends(unit)
    else:
        lax.fori_loop(0, steps, one_step, 0)
        lax.fori_loop(units, units + LAG * (n_row - 1), rest, 0)
        lax.fori_loop(late_from, units, late, 0)

    for copy in smalls[3:]:
        copy.wait()

    part_rows = acc.shape[2]
    per_final = final.shape[1] // part_rows

    def direct_total(u, q, down):
        sent(u, z, z, far_middle).wait_recv()

        @pl.when(is_end)
        def _():
            sent(u, z, z, middle_of).wait_recv()
            final[q, down, :] = (
                acc[u, z] + up_in[u, middle_of].astype(jnp.float32)
            ) + up_in[u, far_middle].astype(jnp.float32)

        @pl.when(jnp.logical_not(is_end))
        def _():
            sent(u, z, z, end_of).wait_recv()
            final[q, down, :] = (
                acc[u, z] + up_in[u, far_middle].astype(jnp.float32)
            ) + up_in[u, end_of].astype(jnp.float32)

    def chain_total(u, q, down):
        @pl.when(z > 0)
        def _():
            passed(u, z, z + 1, True).wait_recv()

        @pl.when(z < n_row - 1)
        def _():
            passed(u, z, z - 1, False).wait_recv()

        @pl.when(z == 0)
        def _():
            final[q, down, :] = acc[u, z] + down_in[u, z].astype(jnp.float32)

        @pl.when(z == n_row - 1)
        def _():
            final[q, down, :] = acc[u, z] + up_in[u, z].astype(jnp.float32)

        @pl.when(jnp.logical_and(z > 0, z < n_row - 1))
        def _():
            final[q, down, :] = (
                acc[u, z] + up_in[u, z].astype(jnp.float32)
            ) + down_in[u, z].astype(jnp.float32)

    def finish(at, carry):
        for k in range(per_final):
            step = at * per_final + k
            for q in range(halves):
                u = step * halves + q
                down = slice(k * part_rows, (k + 1) * part_rows)

                (direct_total if direct else chain_total)(u, q, down)

        hidden = jnp.concatenate(
            [
                jnp.concatenate(
                    [final[q, pl.ds(r, FINAL, own), :] for r in range(own)], axis=0
                )
                for q in range(halves)
            ],
            axis=1,
        ).astype(jnp.bfloat16)
        mixed = jnp.dot(hidden, weight[...], preferred_element_type=jnp.float32) + bias[...]
        mixed = jnp.maximum(mixed, 0.0).astype(jnp.bfloat16)
        for r in range(own):
            out_ref[r, pl.ds(pl.multiple_of(at * FINAL, FINAL), FINAL), :] = mixed[
                r * FINAL : (r + 1) * FINAL
            ]
        return carry

    lax.fori_loop(0, TILE // FINAL, finish, 0)

    for q in range(halves):
        for d in range(1, chips):
            for cut in range(cuts):
                far(d, q, cut).wait_send()
        for d in range(chips):
            for cut in range(cuts):
                near(d, q, cut).wait_send()

    def drain(u, carry):
        if direct:
            for o in range(n_row):

                @pl.when(z != o)
                def _():
                    sent(u, o, o, z).wait_send()

            return carry

        def up_one(o, inner):
            passed(u, o, z + 1, True).wait_send()
            return inner

        def down_one(o, inner):
            passed(u, o, z - 1, False).wait_send()
            return inner

        lax.fori_loop(z + 1, n_row, up_one, 0)
        lax.fori_loop(0, z, down_one, 0)
        return carry

    lax.fori_loop(0, units, drain, 0)


def on_device(features, tile_values, tile_rows, tile_cols, counts, weight, bias):
    n_row, n_col = lax.axis_size("row"), lax.axis_size("col")
    piece_rows, width = features.shape[1:]
    slots, entries = tile_values.shape[2:]
    own = piece_rows // TILE
    row_tiles = n_row * own
    source_rows = n_col * piece_rows
    tiles_in = row_tiles * source_rows // TILE
    steps, held, piece = (4, 4, 512) if n_row == 4 else (16, 1, 256)
    lanes = entries // steps
    blocks = lanes // LANES
    halves = width // LANES
    cuts = 4
    part_rows = 2 * blocks * own
    slabs = (steps * halves, n_row, part_rows, LANES)
    dma = pltpu.SemaphoreType.DMA
    anywhere = pl.BlockSpec(memory_space=pl.ANY)
    out = pl.pallas_call(
        functools.partial(layer_kernel, n_row, n_col, piece),
        in_specs=[anywhere] * 7,
        out_specs=pl.BlockSpec(memory_space=pltpu.VMEM),
        out_shape=jax.ShapeDtypeStruct((own, TILE, width), jnp.bfloat16),
        scratch_shapes=[
            pltpu.VMEM((steps, slots, lanes), jnp.bfloat16),
            pltpu.VMEM((1, 1), jnp.int32),
            pltpu.VMEM((1, slots), jnp.int32),
            pltpu.VMEM((1, slots), jnp.int32),
            pltpu.VMEM((width, width), jnp.bfloat16),
            pltpu.VMEM((1, width), jnp.float32),
            pltpu.VMEM((tiles_in, slots), jnp.bfloat16),
            pltpu.VMEM((held, blocks * row_tiles, 2 * source_rows), jnp.bfloat16),
            pltpu.VMEM((halves, source_rows, LANES), jnp.bfloat16),
            pltpu.VMEM((halves, 2 * source_rows, 2 * LANES), jnp.bfloat16),
            pltpu.VMEM(slabs, jnp.float32),
            pltpu.VMEM(slabs, jnp.bfloat16),
            pltpu.VMEM(slabs, jnp.bfloat16),
            pltpu.VMEM((halves, FINAL * own, LANES), jnp.float32),
            dma((steps,)), dma((5,)), dma((halves,)),
            dma((n_col // 2, halves, cuts)), dma((n_col // 2, halves, cuts)),
            dma((n_col // 2, halves, cuts)), dma((n_col // 2, halves, cuts)),
            dma((steps * halves, n_row)), dma((steps * halves, n_row)),
            dma((steps * halves, n_row)),
        ],
        compiler_params=pltpu.CompilerParams(
            collective_id=0, has_side_effects=True, vmem_limit_bytes=62 * 1024 * 1024
        ),
    )(counts, tile_values, tile_rows, tile_cols, features, weight, bias.reshape(1, width))
    return out.reshape(1, piece_rows, width)


def solution(mesh):
    in_specs = (
        P(("groups", "row"), "col", None),
        P(("groups", "row"), "col", None, None),
        P(("groups", "row"), "col", None),
        P(("groups", "row"), "col", None),
        P(("groups", "row"), "col"),
        P(),
        P(),
    )
    out_specs = P(("groups", "col"), "row", None)
    return jax.shard_map(
        on_device, mesh=mesh, in_specs=in_specs, out_specs=out_specs, check_vma=False
    )
```

time: 40.2 us -> 39.1 us (0.973)
  Pallas kernels: 37.4 us -> 36.6 us
    pallas_call x1, Pallas kernels: 37.4 us -> 36.6 us  [on_device(): pl.pallas_call(functools.partial(layer_kernel, n_row, n_col, piece), in_s...]
where the time goes in v1:
time: 39.1 us; the launch traced here: 38.9 us
  Pallas kernels  36.6 us (94%)
  local copies, waits for them, and re-layouts  1.67 us (4%)
  between operations  0.66 us (2%)
    pallas_call x1, Pallas kernels, on_device(): pl.pallas_call(functools.partial(layer_kernel, n_row, n_col, piece), in_s...  36.6 us
    unnamed x1, local copies, waits for them, and re-layouts  1.67 us

profile of v1, /device:TPU:0, one launch (start us, length us, event | category | flops | bytes accessed | tf_op | source)
XLA Modules:
  0.0 38.9 jit_solution(13832773927423895468)
XLA Ops:
  0.7 36.6 %shard_map.73 = bf16[8,64,256]{2,1,0:T(8,128)(2,1)} custom-call(s32[1,1]{1,0:T(1,128)S(6)} %copy.9.counts_hbm, bf16[1,1,1024,4096]{3,2,1,0:T(8,128)(2,1)} %vals_hbm.1, s32[1,1,1024]{2,1,0:T(1,128)} %rows_hbm.1, s32[1,1,1024]{2,1,0:T(1,128)} %cols_hbm.1, bf16[1,512,256]{2,1,0:T(8,128)(2,1)} %feat_hbm.1, bf16[256,256]{1,0:T(8,128)(2,1)} %weight_hbm.1, ...), custom_call_target="tpu_custom_call" | custom-call | tf_op jit(solution)/shard_map/pallas_call | solution.py:469
  37.3 1.7 %copy.10 = bf16[1,512,256]{2,1,0:T(8,128)(2,1)} copy(bf16[1,512,256]{2,1,0:T(8,128)(2,1)} %bitcast.2) | data formatting | bytes 524288

commit v2 on v1

--- a/solution.py
+++ b/solution.py
@@ -12,17 +12,17 @@
 FINAL = 16
 LAG = 2
 PLAN = (
-    "d00", "d01", "d10", "r00", "d11", "s00", "m00", "x00", "m10", "r10", "x10", "l00",
-    "l10", "d20", "d21", "m20", "x20", "f00", "s10", "m01", "x01", "f10", "m11", "x11",
-    "m21", "x21", "d30", "f20", "d31", "f01", "m30", "x30", "m31", "x31", "f11", "f21",
-    "f30", "f31", "l20", "l01", "l11", "l21", "l30", "l31",
+    "d00", "d01", "D10", "r00", "D11", "s00", "m00", "x00", "r10", "l00", "D20", "s10",
+    "m01", "x01", "f00", "M10", "x10", "x11", "D21", "f01", "M20", "x20", "x21", "f10",
+    "f11", "D30", "f20", "f21", "D31", "M30", "x30", "x31", "f30", "f31", "l10", "l01",
+    "l11", "l20", "l21", "l30", "l31",
 )
 MESH = pl.DeviceIdType.MESH
 
 
 def layer_kernel(
     n_row, n_col, piece, counts_hbm, vals_hbm, rows_hbm, cols_hbm, feat_hbm, weight_hbm, bias_hbm,
-    out_ref, vals, live, rows_in, cols_in, weight, bias, pick, dense, src, wide, acc, up_in, down_in,
+    out_ref, vals, live, rows_in, cols_in, weight, bias, pick, dense, src, wide, whole, acc, up_in, down_in,
     final, vals_sem, small_sem, own_sem, far_send, far_recv, near_send, near_recv, send_sem, up_sem,
     down_sem,
 ):
@@ -142,22 +142,40 @@
             wide[q, pl.ds(low, TILE), part:] = jnp.zeros((TILE, part), jnp.bfloat16)
             wide[q, pl.ds(low + TILE, TILE), :part] = jnp.zeros((TILE, part), jnp.bfloat16)
 
-    def densify(step, held, at_piece):
+    is_low = lax.broadcasted_iota(jnp.int32, (row_tiles, LANES), 1) < TILE
+
+    def densify(step, held, at_piece, turning=False):
         def one_chunk(at, carry):
             first = pl.multiple_of(at * chunk, chunk)
             for low in range(at_piece * piece, (at_piece + 1) * piece, 256):
                 sums = jnp.dot(
                     pick[pl.ds(first, chunk), :], vals[step, :, low : low + 256],
                     preferred_element_type=jnp.float32,
-                ).astype(jnp.bfloat16)
+                )
                 for block in range(2):
                     down = pl.ds((low // LANES + block) * row_tiles, row_tiles)
-                    for c in range(chunk_cols):
-                        lane = pl.multiple_of((at * chunk_cols + c) * LANES, LANES)
-                        dense[held, down, pl.ds(lane, LANES)] = sums[
+
+                    def tiles(c):
+                        return sums[
                             c * row_tiles : (c + 1) * row_tiles,
                             block * LANES : (block + 1) * LANES,
                         ]
+
+                    if turning:
+                        for pair in range(chunk_cols // 2):
+                            even = tiles(2 * pair)
+                            odd = pltpu.roll(tiles(2 * pair + 1), TILE, 1)
+                            lane = pair * LANES
+                            dense[held, down, pl.ds(lane, LANES)] = jnp.where(
+                                is_low, even, odd
+                            ).astype(jnp.bfloat16)
+                            dense[held, down, pl.ds(source_rows + lane, LANES)] = jnp.where(
+                                is_low, odd, even
+                            ).astype(jnp.bfloat16)
+                    else:
+                        for c in range(chunk_cols):
+                            lane = pl.multiple_of((at * chunk_cols + c) * LANES, LANES)
+                            dense[held, down, pl.ds(lane, LANES)] = tiles(c).astype(jnp.bfloat16)
             return carry
 
         if chunk == tiles_in:
@@ -165,9 +183,9 @@
         else:
             lax.fori_loop(0, tiles_in // chunk, one_chunk, 0)
 
-    def relay(q):
+    def relay(q, which=None):
         for d in range(1, chips):
-            for cut in range(cuts):
+            for cut in range(cuts) if which is None else (which,):
                 far(d, q, cut).wait_recv()
                 near(d, q, cut).start()
 
@@ -182,6 +200,10 @@
             low = pl.multiple_of(c * 2 * TILE, 2 * TILE)
             wide[q, pl.ds(low, TILE), :part] = rows
             wide[q, pl.ds(low + TILE, TILE), part:] = rows
+            if direct:
+                other = pl.multiple_of((c + 1 - 2 * lax.rem(c, 2)) * TILE, TILE)
+                whole[0, pl.ds(pl.multiple_of(c * TILE, TILE), TILE), q * part : (q + 1) * part] = rows
+                whole[1, pl.ds(other, TILE), q * part : (q + 1) * part] = rows
 
     def multiply(unit, held, q):
         sums = jnp.dot(dense[held], wide[q], preferred_element_type=jnp.float32)
@@ -194,6 +216,21 @@
                         low : low + own, side * part : (side + 1) * part
                     ]
 
+    def multiply_whole(step, held):
+        for side in range(2):
+            sums = jnp.dot(
+                dense[held, :, side * source_rows : (side + 1) * source_rows], whole[side],
+                preferred_element_type=jnp.float32,
+            )
+            for q in range(halves):
+                for block in range(blocks):
+                    for owner in range(n_row):
+                        low = block * row_tiles + owner * own
+                        to = (2 * block + side) * own
+                        acc[step * halves + q, owner, to : to + own, :] = sums[
+                            low : low + own, q * part : (q + 1) * part
+                        ]
+
     def passed(u, o, to, is_up):
         land, sem = (up_in, up_sem) if is_up else (down_in, down_sem)
         return pltpu.make_async_remote_copy(
@@ -248,9 +285,9 @@
             pass_down(below, 0, jnp.where(below < late_from, below_count, below_early))
 
     is_end = jnp.logical_or(z == 0, z == n_row - 1)
-    is_low = z < 2
-    end_of = jnp.where(is_low, 0, n_row - 1)
-    middle_of = jnp.where(is_low, 1, n_row - 2)
+    is_below = z < 2
+    end_of = jnp.where(is_below, 0, n_row - 1)
+    middle_of = jnp.where(is_below, 1, n_row - 2)
     far_middle = n_row - 1 - middle_of
     far_end = n_row - 1 - end_of
 
@@ -325,6 +362,14 @@
                 if k == 0:
                     load(at).wait()
                 densify(at, at, k)
+            elif what == "D":
+                if k == 0:
+                    load(at).wait()
+                densify(at, at, k, True)
+            elif what == "M":
+                multiply_whole(at, at)
+            elif what == "c":
+                relay(at, k)
             elif what == "r":
                 relay(at)
             elif what == "s":
@@ -465,12 +510,12 @@
     part_rows = 2 * blocks * own
     slabs = (steps * halves, n_row, part_rows, LANES)
     dma = pltpu.SemaphoreType.DMA
-    anywhere = pl.BlockSpec(memory_space=pl.ANY)
+    anywhere = pl.BlockSpec(memory_space=pltpu.HBM)
     out = pl.pallas_call(
         functools.partial(layer_kernel, n_row, n_col, piece),
         in_specs=[anywhere] * 7,
         out_specs=pl.BlockSpec(memory_space=pltpu.VMEM),
-        out_shape=jax.ShapeDtypeStruct((own, TILE, width), jnp.bfloat16),
+        out_shape=pltpu.VMEM((own, TILE, width), jnp.bfloat16),
         scratch_shapes=[
             pltpu.VMEM((steps, slots, lanes), jnp.bfloat16),
             pltpu.VMEM((1, 1), jnp.int32),
@@ -482,6 +527,7 @@
             pltpu.VMEM((held, blocks * row_tiles, 2 * source_rows), jnp.bfloat16),
             pltpu.VMEM((halves, source_rows, LANES), jnp.bfloat16),
             pltpu.VMEM((halves, 2 * source_rows, 2 * LANES), jnp.bfloat16),
+            pltpu.VMEM((2, source_rows if n_row == 4 else TILE, width), jnp.bfloat16),
             pltpu.VMEM(slabs, jnp.float32),
             pltpu.VMEM(slabs, jnp.bfloat16),
             pltpu.VMEM(slabs, jnp.bfloat16),

time: 39.1 us -> 34.9 us (0.89)
  Pallas kernels: 36.6 us -> 33.4 us
  local copies, waits for them, and re-layouts: 1.67 us -> 0.71 us
    pallas_call x1, Pallas kernels: 36.6 us -> 33.4 us  [on_device(): pl.pallas_call(functools.partial(layer_kernel, n_row, n_col, piece), in_s...]
    unnamed x1, local copies, waits for them, and re-layouts: 1.67 us -> 0.71 us
where the time goes in v2:
time: 34.9 us; the launch traced here: 34.7 us
  Pallas kernels  33.4 us (96%)
  local copies, waits for them, and re-layouts  0.71 us (2%)
  between operations  0.66 us (2%)
    pallas_call x1, Pallas kernels, on_device(): pl.pallas_call(functools.partial(layer_kernel, n_row, n_col, piece), in_s...  33.4 us
    unnamed x1, local copies, waits for them, and re-layouts  0.71 us

profile of v2, /device:TPU:0, one launch (start us, length us, event | category | flops | bytes accessed | tf_op | source)
XLA Modules:
  0.0 34.7 jit_solution(550308010960970846)
XLA Ops:
  0.7 33.4 %shard_map.73 = bf16[8,64,256]{2,1,0:T(8,128)(2,1)S(1)} custom-call(s32[1,1]{1,0:T(1,128)S(6)} %copy.10.counts_hbm, bf16[1,1,1024,4096]{3,2,1,0:T(8,128)(2,1)} %vals_hbm.1, s32[1,1,1024]{2,1,0:T(1,128)} %rows_hbm.1, s32[1,1,1024]{2,1,0:T(1,128)} %cols_hbm.1, bf16[1,512,256]{2,1,0:T(8,128)(2,1)} %feat_hbm.1, bf16[256,256]{1,0:T(8,128)(2,1)} %weight_hbm.1, ...), custom_call_target="tpu_custom_call" | custom-call | tf_op jit(solution)/shard_map/pallas_call | solution.py:514
  34.0 0.7 %copy.9 = bf16[1,512,256]{2,1,0:T(8,128)(2,1)} copy(bf16[1,512,256]{2,1,0:T(8,128)(2,1)S(1)} %bitcast.2) | data formatting | bytes 524288

commit v3 on v2

--- a/solution.py
+++ b/solution.py
@@ -12,10 +12,10 @@
 FINAL = 16
 LAG = 2
 PLAN = (
-    "d00", "d01", "D10", "r00", "D11", "s00", "m00", "x00", "r10", "l00", "D20", "s10",
-    "m01", "x01", "f00", "M10", "x10", "x11", "D21", "f01", "M20", "x20", "x21", "f10",
-    "f11", "D30", "f20", "f21", "D31", "M30", "x30", "x31", "f30", "f31", "l10", "l01",
-    "l11", "l20", "l21", "l30", "l31",
+    "d00", "d01", "D10", "r00", "D11", "s00", "m00", "g00", "r10", "n00", "l00", "D20",
+    "s10", "m01", "x01", "f00", "M10", "x10", "x11", "D21", "M20", "x20", "x21", "f01",
+    "f10", "D30", "f11", "f20", "D31", "M30", "x30", "x31", "f21", "f30", "f31", "l10",
+    "l01", "l11", "l20", "l21", "l30", "l31",
 )
 MESH = pl.DeviceIdType.MESH
 
@@ -302,10 +302,14 @@
         down_in[u, o] = acc[u, o].astype(jnp.bfloat16)
         sent(u, o, to, at).start()
 
-    def first_sends(u):
+    def farthest_sends(u):
         @pl.when(is_end)
         def _():
             send(u, far_end, middle_of, middle_of)
+
+    def next_sends(u):
+        @pl.when(is_end)
+        def _():
             send(u, far_middle, middle_of, far_end)
 
         @pl.when(jnp.logical_not(is_end))
@@ -377,7 +381,12 @@
             elif what == "m":
                 multiply(unit, at, k)
             elif what == "x":
-                first_sends(unit)
+                farthest_sends(unit)
+                next_sends(unit)
+            elif what == "g":
+                farthest_sends(unit)
+            elif what == "n":
+                next_sends(unit)
             elif what == "f":
                 forward(unit)
             elif what == "l":
@@ -506,7 +515,7 @@
     lanes = entries // steps
     blocks = lanes // LANES
     halves = width // LANES
-    cuts = 4
+    cuts = 2
     part_rows = 2 * blocks * own
     slabs = (steps * halves, n_row, part_rows, LANES)
     dma = pltpu.SemaphoreType.DMA

time: 34.9 us -> 34.2 us (0.980)
  Pallas kernels: 33.4 us -> 32.7 us
    pallas_call x1, Pallas kernels: 33.4 us -> 32.7 us  [on_device(): pl.pallas_call(functools.partial(layer_kernel, n_row, n_col, piece), in_s...]
where the time goes in v3:
time: 34.2 us; the launch traced here: 34.1 us
  Pallas kernels  32.7 us (96%)
  local copies, waits for them, and re-layouts  0.71 us (2%)
  between operations  0.66 us (2%)
    pallas_call x1, Pallas kernels, on_device(): pl.pallas_call(functools.partial(layer_kernel, n_row, n_col, piece), in_s...  32.7 us
    unnamed x1, local copies, waits for them, and re-layouts  0.71 us

profile of v3, /device:TPU:0, one launch (start us, length us, event | category | flops | bytes accessed | tf_op | source)
XLA Modules:
  0.0 34.1 jit_solution(9717920718779654478)
XLA Ops:
  0.7 32.7 %shard_map.73 = bf16[8,64,256]{2,1,0:T(8,128)(2,1)S(1)} custom-call(s32[1,1]{1,0:T(1,128)S(6)} %copy.10.counts_hbm, bf16[1,1,1024,4096]{3,2,1,0:T(8,128)(2,1)} %vals_hbm.1, s32[1,1,1024]{2,1,0:T(1,128)} %rows_hbm.1, s32[1,1,1024]{2,1,0:T(1,128)} %cols_hbm.1, bf16[1,512,256]{2,1,0:T(8,128)(2,1)} %feat_hbm.1, bf16[256,256]{1,0:T(8,128)(2,1)} %weight_hbm.1, ...), custom_call_target="tpu_custom_call" | custom-call | tf_op jit(solution)/shard_map/pallas_call | solution.py:523
  33.4 0.7 %copy.9 = bf16[1,512,256]{2,1,0:T(8,128)(2,1)} copy(bf16[1,512,256]{2,1,0:T(8,128)(2,1)S(1)} %bitcast.2) | data formatting | bytes 524288

commit v4 on v3

--- a/solution.py
+++ b/solution.py
@@ -11,11 +11,11 @@
 LANES = 128
 FINAL = 16
 LAG = 2
+SPLIT = 1
 PLAN = (
     "d00", "d01", "D10", "r00", "D11", "s00", "m00", "g00", "r10", "n00", "l00", "D20",
-    "s10", "m01", "x01", "f00", "M10", "x10", "x11", "D21", "M20", "x20", "x21", "f01",
-    "f10", "D30", "f11", "f20", "D31", "M30", "x30", "x31", "f21", "f30", "f31", "l10",
-    "l01", "l11", "l20", "l21", "l30", "l31",
+    "s10", "m01", "x01", "f00", "M10", "x10", "D21", "M20", "x20", "f01", "D30", "f10",
+    "D31", "f20", "M30", "x30", "f30", "l01", "l10", "l20", "l30",
 )
 MESH = pl.DeviceIdType.MESH
 
@@ -205,14 +205,14 @@
                 whole[0, pl.ds(pl.multiple_of(c * TILE, TILE), TILE), q * part : (q + 1) * part] = rows
                 whole[1, pl.ds(other, TILE), q * part : (q + 1) * part] = rows
 
-    def multiply(unit, held, q):
+    def multiply(step, held, q):
         sums = jnp.dot(dense[held], wide[q], preferred_element_type=jnp.float32)
         for block in range(blocks):
             for owner in range(n_row):
                 low = block * row_tiles + owner * own
                 for side in range(2):
                     to = (2 * block + side) * own
-                    acc[unit, owner, to : to + own, :] = sums[
+                    acc[step, owner, q, to : to + own, :] = sums[
                         low : low + own, side * part : (side + 1) * part
                     ]
 
@@ -227,32 +227,36 @@
                     for owner in range(n_row):
                         low = block * row_tiles + owner * own
                         to = (2 * block + side) * own
-                        acc[step * halves + q, owner, to : to + own, :] = sums[
+                        acc[step, owner, q, to : to + own, :] = sums[
                             low : low + own, q * part : (q + 1) * part
                         ]
 
     def passed(u, o, to, is_up):
         land, sem = (up_in, up_sem) if is_up else (down_in, down_sem)
         return pltpu.make_async_remote_copy(
-            src_ref=land.at[u, o], dst_ref=land.at[u, o],
+            src_ref=land.at[u // halves, o, u % halves],
+            dst_ref=land.at[u // halves, o, u % halves],
             send_sem=send_sem.at[u, o], recv_sem=sem.at[u, o],
             device_id={"row": to}, device_id_type=MESH,
         )
 
     def pass_on(u, is_first, is_up, to, owner_of, begin, end):
         land = up_in if is_up else down_in
+        p, q = u // halves, u % halves
 
         def one(j, carry):
             o = owner_of(j)
 
             @pl.when(is_first)
             def _():
-                land[u, o] = acc[u, o].astype(jnp.bfloat16)
+                land[p, o, q] = acc[p, o, q].astype(jnp.bfloat16)
 
             @pl.when(jnp.logical_not(is_first))
             def _():
                 passed(u, o, to, is_up).wait_recv()
-                land[u, o] = (acc[u, o] + land[u, o].astype(jnp.float32)).astype(jnp.bfloat16)
+                land[p, o, q] = (
+                    acc[p, o, q] + land[p, o, q].astype(jnp.float32)
+                ).astype(jnp.bfloat16)
 
             passed(u, o, to, is_up).start()
             return carry
@@ -291,16 +295,22 @@
     far_middle = n_row - 1 - middle_of
     far_end = n_row - 1 - end_of
 
-    def sent(u, o, to, at):
+    def place_of(unit, o):
+        p, q = unit
+        return (p, o) if q is None else (p, o, q)
+
+    def sent(unit, o, to, at):
+        p, q = unit
+        u = p * halves + (0 if q is None else q)
         return pltpu.make_async_remote_copy(
-            src_ref=down_in.at[u, o], dst_ref=up_in.at[u, at],
+            src_ref=down_in.at[place_of(unit, o)], dst_ref=up_in.at[place_of(unit, at)],
             send_sem=send_sem.at[u, o], recv_sem=up_sem.at[u, at],
             device_id={"row": to}, device_id_type=MESH,
         )
 
-    def send(u, o, to, at):
-        down_in[u, o] = acc[u, o].astype(jnp.bfloat16)
-        sent(u, o, to, at).start()
+    def send(unit, o, to, at):
+        down_in[place_of(unit, o)] = acc[place_of(unit, o)].astype(jnp.bfloat16)
+        sent(unit, o, to, at).start()
 
     def farthest_sends(u):
         @pl.when(is_end)
@@ -321,8 +331,8 @@
         def _():
             for o, at in ((far_end, z), (far_middle, far_end)):
                 sent(u, far_end, far_end, at).wait_recv()
-                down_in[u, o] = (
-                    acc[u, o] + up_in[u, at].astype(jnp.float32)
+                down_in[place_of(u, o)] = (
+                    acc[place_of(u, o)] + up_in[place_of(u, at)].astype(jnp.float32)
                 ).astype(jnp.bfloat16)
                 sent(u, o, o, z).start()
 
@@ -345,7 +355,7 @@
                 spread(q)
 
         for q in range(halves):
-            multiply(step * halves + q, 0, q)
+            multiply(step, 0, q)
             chain_exchange(step * halves + q)
         return carry
 
@@ -361,7 +371,7 @@
     if direct:
         for action in PLAN:
             what, at, k = action[0], int(action[1]), int(action[2])
-            unit = at * halves + k
+            unit = (at, k if at < SPLIT else None)
             if what == "d":
                 if k == 0:
                     load(at).wait()
@@ -379,7 +389,7 @@
             elif what == "s":
                 spread(at)
             elif what == "m":
-                multiply(unit, at, k)
+                multiply(at, at, k)
             elif what == "x":
                 farthest_sends(unit)
                 next_sends(unit)
@@ -399,57 +409,64 @@
     for copy in smalls[3:]:
         copy.wait()
 
-    part_rows = acc.shape[2]
+    part_rows = acc.shape[3]
     per_final = final.shape[1] // part_rows
 
-    def direct_total(u, q, down):
-        sent(u, z, z, far_middle).wait_recv()
+    def direct_total(unit, to):
+        sent(unit, z, z, far_middle).wait_recv()
+        far_sum = up_in[place_of(unit, far_middle)].astype(jnp.float32)
 
         @pl.when(is_end)
         def _():
-            sent(u, z, z, middle_of).wait_recv()
+            sent(unit, z, z, middle_of).wait_recv()
+            final[to] = (
+                acc[place_of(unit, z)] + up_in[place_of(unit, middle_of)].astype(jnp.float32)
+            ) + far_sum
+
+        @pl.when(jnp.logical_not(is_end))
+        def _():
+            sent(unit, z, z, end_of).wait_recv()
+            final[to] = (
+                acc[place_of(unit, z)] + far_sum
+            ) + up_in[place_of(unit, end_of)].astype(jnp.float32)
+
+    def chain_total(u, q, down):
+        p = u // halves
+
+        @pl.when(z > 0)
+        def _():
+            passed(u, z, z + 1, True).wait_recv()
+
+        @pl.when(z < n_row - 1)
+        def _():
+            passed(u, z, z - 1, False).wait_recv()
+
+        @pl.when(z == 0)
+        def _():
+            final[q, down, :] = acc[p, z, q] + down_in[p, z, q].astype(jnp.float32)
+
+        @pl.when(z == n_row - 1)
+        def _():
+            final[q, down, :] = acc[p, z, q] + up_in[p, z, q].astype(jnp.float32)
+
+        @pl.when(jnp.logical_and(z > 0, z < n_row - 1))
+        def _():
             final[q, down, :] = (
-                acc[u, z] + up_in[u, middle_of].astype(jnp.float32)
-            ) + up_in[u, far_middle].astype(jnp.float32)
-
-        @pl.when(jnp.logical_not(is_end))
-        def _():
-            sent(u, z, z, end_of).wait_recv()
-            final[q, down, :] = (
-                acc[u, z] + up_in[u, far_middle].astype(jnp.float32)
-            ) + up_in[u, end_of].astype(jnp.float32)
-
-    def chain_total(u, q, down):
-        @pl.when(z > 0)
-        def _():
-            passed(u, z, z + 1, True).wait_recv()
-
-        @pl.when(z < n_row - 1)
-        def _():
-            passed(u, z, z - 1, False).wait_recv()
-
-        @pl.when(z == 0)
-        def _():
-            final[q, down, :] = acc[u, z] + down_in[u, z].astype(jnp.float32)
-
-        @pl.when(z == n_row - 1)
-        def _():
-            final[q, down, :] = acc[u, z] + up_in[u, z].astype(jnp.float32)
-
-        @pl.when(jnp.logical_and(z > 0, z < n_row - 1))
-        def _():
-            final[q, down, :] = (
-                acc[u, z] + up_in[u, z].astype(jnp.float32)
-            ) + down_in[u, z].astype(jnp.float32)
-
-    def finish(at, carry):
-        for k in range(per_final):
-            step = at * per_final + k
+                acc[p, z, q] + up_in[p, z, q].astype(jnp.float32)
+            ) + down_in[p, z, q].astype(jnp.float32)
+
+    def finish(at, carry, split=False):
+        if direct and split:
             for q in range(halves):
-                u = step * halves + q
-                down = slice(k * part_rows, (k + 1) * part_rows)
-
-                (direct_total if direct else chain_total)(u, q, down)
+                direct_total((at, q), q)
+        elif direct:
+            direct_total((at, None), slice(None))
+        else:
+            for k in range(per_final):
+                step = at * per_final + k
+                for q in range(halves):
+                    down = slice(k * part_rows, (k + 1) * part_rows)
+                    chain_total(step * halves + q, q, down)
 
         hidden = jnp.concatenate(
             [
@@ -468,7 +485,10 @@
             ]
         return carry
 
-    lax.fori_loop(0, TILE // FINAL, finish, 0)
+    if direct:
+        for at in range(SPLIT):
+            finish(at, 0, True)
+    lax.fori_loop(SPLIT if direct else 0, TILE // FINAL, finish, 0)
 
     for q in range(halves):
         for d in range(1, chips):
@@ -479,15 +499,6 @@
                 near(d, q, cut).wait_send()
 
     def drain(u, carry):
-        if direct:
-            for o in range(n_row):
-
-                @pl.when(z != o)
-                def _():
-                    sent(u, o, o, z).wait_send()
-
-            return carry
-
         def up_one(o, inner):
             passed(u, o, z + 1, True).wait_send()
             return inner
@@ -500,7 +511,24 @@
         lax.fori_loop(0, z, down_one, 0)
         return carry
 
-    lax.fori_loop(0, units, drain, 0)
+    def drain_direct(unit):
+        for o in range(n_row):
+
+            @pl.when(z != o)
+            def _():
+                sent(unit, o, o, z).wait_send()
+
+    def drain_whole(p, carry):
+        drain_direct((p, None))
+        return carry
+
+    if direct:
+        for p in range(SPLIT):
+            for q in range(halves):
+                drain_direct((p, q))
+        lax.fori_loop(SPLIT, steps, drain_whole, 0)
+    else:
+        lax.fori_loop(0, units, drain, 0)
 
 
 def on_device(features, tile_values, tile_rows, tile_cols, counts, weight, bias):
@@ -517,7 +545,7 @@
     halves = width // LANES
     cuts = 2
     part_rows = 2 * blocks * own
-    slabs = (steps * halves, n_row, part_rows, LANES)
+    slabs = (steps, n_row, halves, part_rows, LANES)
     dma = pltpu.SemaphoreType.DMA
     anywhere = pl.BlockSpec(memory_space=pltpu.HBM)
     out = pl.pallas_call(

time: 34.2 us -> 33.9 us (level)
  Pallas kernels: 32.7 us -> 32.3 us
    pallas_call x1, Pallas kernels: 32.7 us -> 32.3 us  [on_device(): pl.pallas_call(functools.partial(layer_kernel, n_row, n_col, piece), in_s...]
where the time goes in v4:
time: 33.9 us; the launch traced here: 33.7 us
  Pallas kernels  32.3 us (95%)
  local copies, waits for them, and re-layouts  0.71 us (2%)
  between operations  0.66 us (2%)
    pallas_call x1, Pallas kernels, on_device(): pl.pallas_call(functools.partial(layer_kernel, n_row, n_col, piece), in_s...  32.3 us
    unnamed x1, local copies, waits for them, and re-layouts  0.71 us

profile of v4, /device:TPU:0, one launch (start us, length us, event | category | flops | bytes accessed | tf_op | source)
XLA Modules:
  0.0 33.7 jit_solution(12971709574157772916)
XLA Ops:
  0.7 32.3 %shard_map.73 = bf16[8,64,256]{2,1,0:T(8,128)(2,1)S(1)} custom-call(s32[1,1]{1,0:T(1,128)S(6)} %copy.10.counts_hbm, bf16[1,1,1024,4096]{3,2,1,0:T(8,128)(2,1)} %vals_hbm.1, s32[1,1,1024]{2,1,0:T(1,128)} %rows_hbm.1, s32[1,1,1024]{2,1,0:T(1,128)} %cols_hbm.1, bf16[1,512,256]{2,1,0:T(8,128)(2,1)} %feat_hbm.1, bf16[256,256]{1,0:T(8,128)(2,1)} %weight_hbm.1, ...), custom_call_target="tpu_custom_call" | custom-call | tf_op jit(solution)/shard_map/pallas_call | solution.py:551
  33.0 0.7 %copy.9 = bf16[1,512,256]{2,1,0:T(8,128)(2,1)} copy(bf16[1,512,256]{2,1,0:T(8,128)(2,1)S(1)} %bitcast.2) | data formatting | bytes 524288

commit v5 on v4

--- a/solution.py
+++ b/solution.py
@@ -14,7 +14,7 @@
 SPLIT = 1
 PLAN = (
     "d00", "d01", "D10", "r00", "D11", "s00", "m00", "g00", "r10", "n00", "l00", "D20",
-    "s10", "m01", "x01", "f00", "M10", "x10", "D21", "M20", "x20", "f01", "D30", "f10",
+    "s10", "m01", "x01", "M10", "x10", "f00", "D21", "M20", "x20", "f01", "D30", "f10",
     "D31", "f20", "M30", "x30", "f30", "l01", "l10", "l20", "l30",
 )
 MESH = pl.DeviceIdType.MESH

time: 33.9 us -> 33.9 us (level)
  no operation moved by 1% of the time
where the time goes in v5:
time: 33.9 us; the launch traced here: 33.7 us
  Pallas kernels  32.3 us (95%)
  local copies, waits for them, and re-layouts  0.71 us (2%)
  between operations  0.66 us (2%)
    pallas_call x1, Pallas kernels, on_device(): pl.pallas_call(functools.partial(layer_kernel, n_row, n_col, piece), in_s...  32.3 us
    unnamed x1, local copies, waits for them, and re-layouts  0.71 us

profile of v5, /device:TPU:0, one launch (start us, length us, event | category | flops | bytes accessed | tf_op | source)
XLA Modules:
  0.0 33.7 jit_solution(7472376667590356056)
XLA Ops:
  0.7 32.3 %shard_map.73 = bf16[8,64,256]{2,1,0:T(8,128)(2,1)S(1)} custom-call(s32[1,1]{1,0:T(1,128)S(6)} %copy.10.counts_hbm, bf16[1,1,1024,4096]{3,2,1,0:T(8,128)(2,1)} %vals_hbm.1, s32[1,1,1024]{2,1,0:T(1,128)} %rows_hbm.1, s32[1,1,1024]{2,1,0:T(1,128)} %cols_hbm.1, bf16[1,512,256]{2,1,0:T(8,128)(2,1)} %feat_hbm.1, bf16[256,256]{1,0:T(8,128)(2,1)} %weight_hbm.1, ...), custom_call_target="tpu_custom_call" | custom-call | tf_op jit(solution)/shard_map/pallas_call | solution.py:551
  33.0 0.7 %copy.9 = bf16[1,512,256]{2,1,0:T(8,128)(2,1)} copy(bf16[1,512,256]{2,1,0:T(8,128)(2,1)S(1)} %bitcast.2) | data formatting | bytes 524288
